TPU v7x, 32 devices: a whole 2x2x4 slice. The times are simulated.
32 devices in a mesh: groups: 2 (over y), seq: 8 (over z, x), branch: 2 (over core).
Axes of the slice: x: 2, y: 2, z: 4, core: 2. Of those that a mesh axis runs over, the one named last changes fastest.
Arguments:
- queries: bfloat16 [2, 256, 1536], P('branch', ('groups', 'seq')), parts along dimension 1, may hold values from -8 to 8
- key_rows: bfloat16 [2, 256, 1536], P('branch', ('groups', 'seq')), parts along dimension 1, may hold values from -8 to 8
- value_rows: bfloat16 [2, 256, 1536], P('branch', ('groups', 'seq')), parts along dimension 1, may hold values from -40 to 40
- counts: int32 [16], P('groups'), parts along dimension 0, may hold values from 1 to 16, 112 in all
- head_of: int32 [8, 2], replicated, may hold values from 0 to 11, as said below
- out_weight: bfloat16 [1536, 1536], P(None, 'branch'), may hold values from -0.15625 to 0.15625
Outputs:
- projected: bfloat16 [256, 1536], P(('groups', 'seq'), 'branch'), parts along dimension 0
- saved_logsumexp: float32 [2, 16, 2, 16, 8], P('branch', ('groups', 'seq')), parts along dimension 1
There are 2 independent parts, one for each index of `groups`. A program takes and returns all parts, laid end to end along the dimension named above; an argument that names none is the same for every part. Nothing has to cross between parts.
Inputs may be any that keep to these rules, and one draw needn't show every extreme that they name: `head_of`: each of the 12 heads is named by at least 1 entries, and one head by exactly 1.
All inputs are finite; a program needn't handle non-finite values. Where the computation divides by a largest or mean magnitude, that divisor is 1e-20 or more.
Results may differ from a plain program's by a relative error of at most 0.0063.
Values may be sent and summed in bfloat16 or wider, within the bound.
No kernel may reach another device: no remote copies, remote signals or barrier semaphores. Data moves between devices by JAX's collectives and lax.ppermute only.
A program may use at most 64 MiB of HBM per device.

v0:
```python
import math

import jax
import jax.numpy as jnp
from jax import lax
from jax.sharding import PartitionSpec as P

HEADS = 12
HDIM = 128


GUIDE_SCALE = 3.0
EPSILON = 1e-06


def partner_2(array, axis, stride):
    return lax.ppermute(array, axis, [(i, i ^ 1 << stride) for i in range(lax.axis_size(axis))])


def slot_layout(head_of):
    flat_heads = head_of.reshape(-1)
    slot_order = jnp.arange(flat_heads.shape[0], dtype=jnp.int32)
    same_head = flat_heads[:, None] == flat_heads[None, :]
    group_size = jnp.sum(same_head.astype(jnp.int32), axis=1)
    earlier = same_head & (slot_order[None, :] < slot_order[:, None])
    group_rank = jnp.sum(earlier.astype(jnp.int32), axis=1)
    return (flat_heads, group_size, group_rank)


def key_grouping(seq_count, tok_dev):
    shard_limit = max(1, 2048 // tok_dev)
    grouping = 1
    for attempt in range(16):
        if grouping * 2 <= shard_limit and seq_count % (grouping * 2) == 0:
            grouping = grouping * 2
    return grouping


def attend_rows(query_block, key_slot, value_slot, key_valid, key_block):
    row_count = query_block.shape[0]
    head_size = query_block.shape[1]
    block_count = key_slot.shape[0] // key_block
    scale_factor = 1.0 / math.sqrt(head_size)

    def fold_block(block_id, state_in):
        top_score, weight_sum, summed = state_in
        scores = (
            jnp.einsum("qd,kd->qk", query_block, key_slot, preferred_element_type=jnp.float32)
            * scale_factor
        )
        scores = jnp.where(key_valid[None, :], scores, -jnp.inf)
        new_top = jnp.maximum(top_score, jnp.max(scores, axis=1))
        fading = jnp.exp(top_score - new_top)
        weights = jnp.exp(scores - new_top[:, None])
        weight_sum = weight_sum * fading + jnp.sum(weights, axis=1)
        summed = summed * fading[:, None] + jnp.dot(
            weights.astype(jnp.bfloat16), value_slot, preferred_element_type=jnp.float32
        )
        return (new_top, weight_sum, summed)

    start_state = (
        jnp.full((row_count,), -jnp.inf, jnp.float32),
        jnp.zeros((row_count,), jnp.float32),
        jnp.zeros((row_count, head_size), jnp.float32),
    )
    top_score, weight_sum, summed = lax.fori_loop(0, block_count, fold_block, start_state)
    return (summed / weight_sum[:, None], top_score + jnp.log(weight_sum))


def serve_slots(query_items, mask_items, key_recv, value_recv, key_valid, key_block):
    source_count, slot_count, item_count, head_size = query_items.shape
    all_tokens = key_recv.shape[0] * key_recv.shape[2]
    per_block = max(1, 512 // source_count)
    slot_outputs = []
    slot_logsum = []
    for slot_id in range(slot_count):
        key_slot = key_recv[:, slot_id].reshape(all_tokens, head_size)
        value_slot = value_recv[:, slot_id].reshape(all_tokens, head_size)
        taken_items = min(per_block, item_count)
        query_block = query_items[:, slot_id, 0:taken_items].reshape(
            source_count * taken_items, head_size
        )
        attended, logsum = attend_rows(query_block, key_slot, value_slot, key_valid, key_block)
        pieces_out = attended.reshape(source_count, taken_items, head_size)
        pieces_sum = logsum.reshape(source_count, taken_items)
        slot_outputs.append(pieces_out)
        slot_logsum.append(pieces_sum)
    attended = jnp.stack(slot_outputs, axis=1)
    logsum = jnp.stack(slot_logsum, axis=1)
    keep_rows = mask_items > 0
    attended = jnp.where(keep_rows[:, :, :, None], attended, 0.0).astype(jnp.bfloat16)
    logsum = jnp.where(keep_rows, logsum, 0.0)
    return (attended, logsum)


def per_device(queries, key_rows, value_rows, counts, head_of, out_weight):
    seq_count = lax.axis_size("seq")
    tok_dev = queries.shape[1]
    slot_count = head_of.shape[1]
    fewest = max(1, seq_count * slot_count // (2 * HEADS))
    row_cap = (tok_dev + fewest - 1) // fewest
    my_index = lax.axis_index("seq")
    flat_heads, group_size, group_rank = slot_layout(head_of)
    row_steps = jnp.arange(row_cap, dtype=jnp.int32)
    served_rows = group_rank[:, None] + group_size[:, None] * row_steps[None, :]
    my_count = counts[my_index]
    clipped = jnp.minimum(served_rows, tok_dev - 1)
    query_grid = queries[0].reshape(tok_dev, HEADS, HDIM)
    row_live = served_rows < my_count
    query_send = query_grid[clipped, flat_heads[:, None]]
    query_send = jnp.where(row_live[:, :, None], query_send, jnp.zeros((), jnp.bfloat16)).reshape(
        seq_count, slot_count, row_cap, HDIM
    )
    mask_send = row_live.astype(jnp.bfloat16).reshape(seq_count, slot_count, row_cap)
    token_ids = jnp.arange(tok_dev, dtype=jnp.int32)
    key_grid = key_rows[0].reshape(tok_dev, HEADS, HDIM)
    value_grid = value_rows[0].reshape(tok_dev, HEADS, HDIM)
    key_send = key_grid[token_ids[None, :], flat_heads[:, None]].reshape(
        seq_count, slot_count, tok_dev, HDIM
    )
    value_send = value_grid[token_ids[None, :], flat_heads[:, None]].reshape(
        seq_count, slot_count, tok_dev, HDIM
    )
    key_valid = (token_ids[None, :] < counts[:, None]).reshape(-1)
    key_block = tok_dev * key_grouping(seq_count, tok_dev)
    query_recv, mask_recv, key_recv, value_recv = (
        lax.all_to_all(query_send, "seq", split_axis=0, concat_axis=0, tiled=True),
        lax.all_to_all(mask_send, "seq", split_axis=0, concat_axis=0, tiled=True),
        lax.all_to_all(key_send, "seq", split_axis=0, concat_axis=0, tiled=True),
        lax.all_to_all(value_send, "seq", split_axis=0, concat_axis=0, tiled=True),
    )
    attended, logsum = serve_slots(
        query_recv, mask_recv, key_recv, value_recv, key_valid, key_block
    )
    returned = lax.all_to_all(attended, "seq", split_axis=0, concat_axis=0, tiled=True)
    head_ids = jnp.arange(HEADS, dtype=jnp.int32)
    head_group = jnp.sum((flat_heads[None, :] == head_ids[:, None]).astype(jnp.int32), axis=1)
    row_rank = token_ids[:, None] % head_group[None, :]
    row_step = token_ids[:, None] // head_group[None, :]
    slot_ids = jnp.arange(flat_heads.shape[0], dtype=jnp.int32)
    matched = (flat_heads[None, None, :] == head_ids[None, :, None]) & (
        group_rank[None, None, :] == row_rank[:, :, None]
    )
    owner_slot = jnp.sum(jnp.where(matched, slot_ids[None, None, :], 0), axis=2)
    flat_index = owner_slot * row_cap + row_step
    returned_rows = returned.reshape(-1, HDIM)
    attended_home = returned_rows[flat_index].reshape(tok_dev, HEADS * HDIM)
    partner = partner_2(attended_home, "branch", 0)
    on_positive = lax.axis_index("branch") == 0
    own_value = attended_home.astype(jnp.float32)
    partner_value = partner.astype(jnp.float32)
    positive = jnp.where(on_positive, own_value, partner_value)
    negative = jnp.where(on_positive, partner_value, own_value)
    guided = GUIDE_SCALE * positive - (GUIDE_SCALE - 1.0) * negative
    magnitude = jnp.mean(jnp.abs(guided), axis=1, keepdims=True)
    normed = (guided / (magnitude + EPSILON)).astype(jnp.bfloat16)
    projected = jnp.dot(normed, out_weight, preferred_element_type=jnp.float32).astype(jnp.bfloat16)
    saved_rows = jnp.transpose(logsum, (1, 2, 0)).reshape(1, 1, slot_count, row_cap, seq_count)
    return (projected, saved_rows)


def solution(mesh):
    return jax.shard_map(
        per_device,
        mesh=mesh,
        in_specs=(
            P("branch", ("groups", "seq"), None),
            P("branch", ("groups", "seq"), None),
            P("branch", ("groups", "seq"), None),
            P("groups"),
            P(),
            P(None, "branch"),
        ),
        out_specs=(
            P(("groups", "seq"), "branch"),
            P("branch", ("groups", "seq"), None, None, None),
        ),
        check_vma=False,
    )
```

profile of v0, /device:TPU:0, one launch (start us, length us, event | category | flops | bytes accessed | tf_op | source)
XLA Modules:
  0.0 70.5 jit_solution(15671144225890329642)
XLA Ops:
  0.6 0.0 copy-start
  0.6 0.9 %copy.29 = s32[8,2]{1,0:T(8,128)S(1)} copy(s32[8,2]{0,1:T(2,128)} %param.10) | data formatting | bytes 128 | tf_op args[4]
  1.5 0.1 eq.69
  1.6 0.2 convert_reduce_fusion.1
  1.8 0.1 mul.120
  1.9 0.1 add.170
  2.0 0.1 fusion.24
  2.1 0.9 %reshape_squeeze.27 = bf16[16,12,128]{2,1,0:T(8,128)(2,1)S(1)} reshape(bf16[1,16,1536]{2,1,0:T(8,128)(2,1)} %param.6) | data formatting | bytes 98304 | tf_op jit(solution)/shard_map/reshape;squeeze | solution.py:108
  3.0 0.1 reshape.510
  3.0 1.6 %gather_fusion = bf16[256,128]{1,0:T(8,128)(2,1)S(1)} fusion(bf16[16,12,128]{2,0,1:T(8,128)(2,1)S(1)} %copy.32, s32[256]{0:T(256)S(1)} %reshape.510), kind=kCustom, calls=%fused_computation | custom fusion | bytes 133120 | tf_op jit(solution)/shard_map/gather | solution.py:110
  4.6 1.2 %dynamic_slice.3 = s32[1]{0:T(128)} dynamic-slice(s32[8]{0:T(128)} %param.9, s32[]{:T(128)S(6)} %select_n.105), dynamic_slice_sizes={1} | dynamic-slice | bytes 12 | tf_op jit(solution)/shard_map/dynamic_slice | solution.py:106
  5.9 1.3 %fusion.37 = (bf16[8,2,16]{2,1,0:T(2,128)(2,1)}, pred[8,2,16]{2,1,0:T(4,128)(4,1)S(1)}) fusion(s32[]{:T(128)} %bitcast, s32[8,2]{1,0:T(8,128)S(1)} %mul.120, s32[8,2]{1,0:T(8,128)S(1)} %add.170), kind=kLoop, calls=%fused_computation.80 | loop fusion | flops 1024 | bytes 900 | tf_op jit(solution)/shard_map/convert_element_type | solution.py:114
  7.2 0.7 %broadcast_select_fusion = bf16[8,2,16,128]{3,2,1,0:T(8,128)(2,1)} fusion(bf16[8,2,16,128]{3,2,1,0:T(8,128)(2,1)S(1)} %bitcast.37, pred[8,2,16]{2,1,0:T(4,128)(4,1)S(1)} %get-tuple-element.39), kind=kLoop, calls=%fused_computation.25 | loop fusion | flops 32768 | bytes 131328 | tf_op jit(solution)/shard_map/jit(_where)/select_n | solution.py:111
  7.9 7.3 %all-to-all-start.1 = ((bf16[8,2,16,128]{3,2,1,0:T(8,128)(2,1)}), bf16[8,2,16,128]{3,2,1,0:T(8,128)(2,1)S(1)}, u32[]{:S(2)}, u32[]{:S(2)}) async-start(bf16[8,2,16,128]{3,2,1,0:T(8,128)(2,1)} %broadcast_select_fusion), calls=%async_computation.1 | async-start | bytes 131072 | tf_op jit(solution)/shard_map/all_to_all | solution.py:127
  15.2 0.7 %iota_compare_fusion.2 = pred[8,16]{1,0:T(8,128)(4,1)S(1)} fusion(s32[8]{0:T(128)} %param.9), kind=kLoop, calls=%fused_computation.66 | loop fusion | flops 128 | bytes 160 | tf_op jit(solution)/shard_map/lt | solution.py:124
  15.9 0.1 convert_reduce_fusion
  16.1 0.9 %reshape_squeeze.31 = bf16[16,12,128]{2,1,0:T(8,128)(2,1)S(1)} reshape(bf16[1,16,1536]{2,1,0:T(8,128)(2,1)} %param.8) | data formatting | bytes 98304 | tf_op jit(solution)/shard_map/reshape;squeeze | solution.py:117
  16.9 0.1 reshape.516
  17.0 0.9 %reshape_squeeze.29 = bf16[16,12,128]{2,1,0:T(8,128)(2,1)S(1)} reshape(bf16[1,16,1536]{2,1,0:T(8,128)(2,1)} %param.7) | data formatting | bytes 98304 | tf_op jit(solution)/shard_map/reshape;squeeze | solution.py:116
  17.9 2.2 %gather_fusion.2 = bf16[256,128]{1,0:T(8,128)(2,1)} fusion(bf16[16,12,128]{2,0,1:T(8,128)(2,1)S(1)} %copy.34, s32[256]{0:T(256)S(1)} %reshape.516), kind=kCustom, calls=%fused_computation.2 | custom fusion | bytes 133120 | tf_op jit(solution)/shard_map/gather | solution.py:121
  20.1 2.2 %gather_fusion.1 = bf16[256,128]{1,0:T(8,128)(2,1)} fusion(bf16[16,12,128]{2,0,1:T(8,128)(2,1)S(1)} %copy.33, s32[256]{0:T(256)S(1)} %reshape.516), kind=kCustom, calls=%fused_computation.1 | custom fusion | bytes 133120 | tf_op jit(solution)/shard_map/gather | solution.py:118
  22.3 0.1 lt.114
  22.4 0.2 add_select_fusion.1
  22.6 0.4 select_reduce_fusion
  22.9 0.0 all-to-all-done.1
  23.0 6.0 %all-to-all-start.2 = ((bf16[8,2,16,128]{3,2,1,0:T(8,128)(2,1)}), bf16[8,2,16,128]{3,2,1,0:T(8,128)(2,1)S(1)}, u32[]{:S(2)}, u32[]{:S(2)}) async-start(bf16[8,2,16,128]{3,2,1,0:T(8,128)(2,1)} %bitcast.3), calls=%async_computation.2 | async-start | bytes 131072 | tf_op jit(solution)/shard_map/all_to_all | solution.py:129
  29.0 6.9 %all-to-all-done.2 = bf16[8,2,16,128]{3,2,1,0:T(8,128)(2,1)S(1)} async-done(((bf16[8,2,16,128]{3,2,1,0:T(8,128)(2,1)}), bf16[8,2,16,128]{3,2,1,0:T(8,128)(2,1)S(1)}, u32[]{:S(2)}, u32[]{:S(2)}) %all-to-all-start.2) | async-done | bytes 65568 | tf_op jit(solution)/shard_map/all_to_all | solution.py:129
  35.9 3.3 %all-to-all-start = ((bf16[8,2,16]{2,1,0:T(2,128)(2,1)}), bf16[8,2,16]{2,1,0:T(2,128)(2,1)S(1)}, u32[]{:S(2)}, u32[]{:S(2)}) async-start(bf16[8,2,16]{2,1,0:T(2,128)(2,1)} %get-tuple-element.38), calls=%async_computation | async-start | bytes 8192 | tf_op jit(solution)/shard_map/all_to_all | solution.py:128
  39.2 0.2 fusion.42
  39.4 0.1 reduce_max.27
  39.5 0.2 fusion.43
  39.7 0.1 reduce_max.26
  39.8 0.1 reduce_sum.77
  39.9 0.1 reduce_sum.76
  40.0 5.5 %all-to-all-done = bf16[8,2,16]{2,1,0:T(2,128)(2,1)S(1)} async-done(((bf16[8,2,16]{2,1,0:T(2,128)(2,1)}), bf16[8,2,16]{2,1,0:T(2,128)(2,1)S(1)}, u32[]{:S(2)}, u32[]{:S(2)}) %all-to-all-start) | async-done | bytes 544 | tf_op jit(solution)/shard_map/all_to_all | solution.py:128
  45.5 3.3 %all-to-all-start.3 = ((bf16[8,2,16,128]{3,2,1,0:T(8,128)(2,1)}), bf16[8,2,16,128]{3,2,1,0:T(8,128)(2,1)S(1)}, u32[]{:S(2)}, u32[]{:S(2)}) async-start(bf16[8,2,16,128]{3,2,1,0:T(8,128)(2,1)} %bitcast.5), calls=%async_computation.3 | async-start | bytes 131072 | tf_op jit(solution)/shard_map/all_to_all | solution.py:130
  48.9 0.6 fusion.25
  49.5 6.2 %all-to-all-done.3 = bf16[8,2,16,128]{3,2,1,0:T(8,128)(2,1)S(1)} async-done(((bf16[8,2,16,128]{3,2,1,0:T(8,128)(2,1)}), bf16[8,2,16,128]{3,2,1,0:T(8,128)(2,1)S(1)}, u32[]{:S(2)}, u32[]{:S(2)}) %all-to-all-start.3) | async-done | bytes 65568 | tf_op jit(solution)/shard_map/all_to_all | solution.py:130
  55.7 0.2 fusion
  55.9 0.2 fusion.2
  56.1 0.7 %fusion.4 = bf16[8,2,16,128]{3,2,1,0:T(8,128)(2,1)} fusion(bf16[8,1,16,128]{3,2,1,0:T(8,128)(2,1)S(1)} %bitcast.43, bf16[8,1,16,128]{3,2,1,0:T(8,128)(2,1)S(1)} %bitcast.45, pred[8,2,16]{2,1,0:T(4,128)(4,1)S(1)} %copy.31), kind=kLoop, calls=%fused_computation.14 | loop fusion | flops 163840 | bytes 131328 | tf_op jit(solution)/shard_map/convert_element_type | solution.py:91
  56.8 3.3 %all-to-all-start.4 = ((bf16[8,2,16,128]{3,2,1,0:T(8,128)(2,1)}), bf16[8,2,16,128]{3,2,1,0:T(8,128)(2,1)S(1)}, u32[]{:S(2)}, u32[]{:S(2)}) async-start(bf16[8,2,16,128]{3,2,1,0:T(8,128)(2,1)} %fusion.4), calls=%async_computation.4 | async-start | bytes 131072 | tf_op jit(solution)/shard_map/all_to_all | solution.py:135
  60.2 0.2 compare_select_fusion
  60.4 0.1 copy.37
  60.5 0.1 reshape.530
  60.6 6.5 %all-to-all-done.4 = bf16[8,2,16,128]{3,2,1,0:T(8,128)(2,1)S(1)} async-done(((bf16[8,2,16,128]{3,2,1,0:T(8,128)(2,1)}), bf16[8,2,16,128]{3,2,1,0:T(8,128)(2,1)S(1)}, u32[]{:S(2)}, u32[]{:S(2)}) %all-to-all-start.4) | async-done | bytes 65568 | tf_op jit(solution)/shard_map/all_to_all | solution.py:135
  67.0 0.8 %gather_fusion.3 = bf16[192,128]{1,0:T(8,128)(2,1)S(1)} fusion(bf16[256,128]{1,0:T(8,128)(2,1)S(1)} %bitcast.36, s32[1024]{0:T(1024)S(1)} %pad_clamp_fusion), kind=kCustom, calls=%fused_computation.3 | custom fusion | bytes 99072 | tf_op jit(solution)/shard_map/gather | solution.py:147
  67.8 0.1 reshape.508
  67.9 0.1 collective-permute-start
  68.0 1.2 %collective-permute-done = bf16[16,1536]{1,0:T(8,128)(2,1)S(1)} collective-permute-done((bf16[16,1536]{1,0:T(8,128)(2,1)S(1)}, bf16[16,1536]{1,0:T(8,128)(2,1)S(1)}, u32[]{:S(2)}, u32[]{:S(2)}) %collective-permute-start) | collective-permute-done | bytes 49184 | tf_op jit(solution)/shard_map/ppermute | solution.py:17
  69.2 0.1 abs_reduce_fusion
  69.4 0.0 copy-done
  69.4 1.1 %convolution_convert_fusion = bf16[16,768]{1,0:T(8,128)(2,1)} fusion(bf16[1536,768]{1,0:T(8,128)(2,1)S(1)} %copy-done, bf16[16,1536]{1,0:T(8,128)(2,1)S(1)} %collective-permute-done, bf16[16,1536]{1,0:T(8,128)(2,1)S(1)} %reshape.508, f32[16]{0:T(128)S(1)} %multiply_add_fusion, pred[]{:T(512)S(6)} %eq.68), kind=kOutput, calls=%fused_computation.12 | convolution fusion | flops 37982208 | bytes 2482241 | tf_op jit(solution)/shard_map/dot_general | solution.py:157
  (19 shorter events, 0.2 us)
Async XLA Ops:
  0.6 68.7 %copy-start = (bf16[1536,768]{1,0:T(8,128)(2,1)S(1)}, bf16[1536,768]{1,0:T(8,128)(2,1)}, u32[]{:S(2)}) copy-start(bf16[1536,768]{1,0:T(8,128)(2,1)} %param.11) | copy-start | bytes 7077892
  7.9 15.0 %all-to-all-start.1 = ((bf16[8,2,16,128]{3,2,1,0:T(8,128)(2,1)}), bf16[8,2,16,128]{3,2,1,0:T(8,128)(2,1)S(1)}, u32[]{:S(2)}, u32[]{:S(2)}) async-start(bf16[8,2,16,128]{3,2,1,0:T(8,128)(2,1)} %broadcast_select_fusion), calls=%async_computation.1 | async-start | bytes 131072 | tf_op jit(solution)/shard_map/all_to_all | solution.py:127
  23.0 12.9 %all-to-all-start.2 = ((bf16[8,2,16,128]{3,2,1,0:T(8,128)(2,1)}), bf16[8,2,16,128]{3,2,1,0:T(8,128)(2,1)S(1)}, u32[]{:S(2)}, u32[]{:S(2)}) async-start(bf16[8,2,16,128]{3,2,1,0:T(8,128)(2,1)} %bitcast.3), calls=%async_computation.2 | async-start | bytes 131072 | tf_op jit(solution)/shard_map/all_to_all | solution.py:129
  35.9 9.6 %all-to-all-start = ((bf16[8,2,16]{2,1,0:T(2,128)(2,1)}), bf16[8,2,16]{2,1,0:T(2,128)(2,1)S(1)}, u32[]{:S(2)}, u32[]{:S(2)}) async-start(bf16[8,2,16]{2,1,0:T(2,128)(2,1)} %get-tuple-element.38), calls=%async_computation | async-start | bytes 8192 | tf_op jit(solution)/shard_map/all_to_all | solution.py:128
  45.5 10.2 %all-to-all-start.3 = ((bf16[8,2,16,128]{3,2,1,0:T(8,128)(2,1)}), bf16[8,2,16,128]{3,2,1,0:T(8,128)(2,1)S(1)}, u32[]{:S(2)}, u32[]{:S(2)}) async-start(bf16[8,2,16,128]{3,2,1,0:T(8,128)(2,1)} %bitcast.5), calls=%async_computation.3 | async-start | bytes 131072 | tf_op jit(solution)/shard_map/all_to_all | solution.py:130
  56.8 10.2 %all-to-all-start.4 = ((bf16[8,2,16,128]{3,2,1,0:T(8,128)(2,1)}), bf16[8,2,16,128]{3,2,1,0:T(8,128)(2,1)S(1)}, u32[]{:S(2)}, u32[]{:S(2)}) async-start(bf16[8,2,16,128]{3,2,1,0:T(8,128)(2,1)} %fusion.4), calls=%async_computation.4 | async-start | bytes 131072 | tf_op jit(solution)/shard_map/all_to_all | solution.py:135
  67.9 1.3 %collective-permute-start = (bf16[16,1536]{1,0:T(8,128)(2,1)S(1)}, bf16[16,1536]{1,0:T(8,128)(2,1)S(1)}, u32[]{:S(2)}, u32[]{:S(2)}) collective-permute-start(bf16[16,1536]{1,0:T(8,128)(2,1)S(1)} %reshape.508), channel_id=1, source_target_pairs={{0,1},{1,0},{2,3},{3,2},{4,5},{5,4},{6,7},{7,6},{8,9},{9,8},{10,11... | collective-permute-start | bytes 147464 | tf_op jit(solution)/shard_map/ppermute | solution.py:17
where the time goes:
time: 71.1 us; the launch traced here: 70.5 us
  waiting for transfers between devices  26.3 us (37%)
  starting transfers between devices  23.3 us (33%)
  local copies, waits for them, and re-layouts  12.6 us (18%)
  other arithmetic  5.54 us (8%)
  matrix products  1.82 us (3%)
  between operations  0.84 us (1%)
    all_to_all x1, starting transfers between devices, per_device(): lax.all_to_all(query_send, 'seq', split_axis=0, concat_axis=0, tiled=True)  7.25 us
    all_to_all x1, waiting for transfers between devices, per_device(): lax.all_to_all(key_send, 'seq', split_axis=0, concat_axis=0, tiled=True)  6.9 us
    all_to_all x1, waiting for transfers between devices, per_device(): lax.all_to_all(attended, 'seq', split_axis=0, concat_axis=0, tiled=True)  6.46 us
    all_to_all x1, waiting for transfers between devices, per_device(): lax.all_to_all(value_send, 'seq', split_axis=0, concat_axis=0, tiled=True)  6.22 us
    all_to_all x1, starting transfers between devices, per_device(): lax.all_to_all(key_send, 'seq', split_axis=0, concat_axis=0, tiled=True)  6.01 us
    all_to_all x1, waiting for transfers between devices, per_device(): lax.all_to_all(mask_send, 'seq', split_axis=0, concat_axis=0, tiled=True)  5.5 us
    all_to_all x1, starting transfers between devices, per_device(): lax.all_to_all(value_send, 'seq', split_axis=0, concat_axis=0, tiled=True)  3.35 us
    all_to_all x1, starting transfers between devices, per_device(): lax.all_to_all(attended, 'seq', split_axis=0, concat_axis=0, tiled=True)  3.35 us
  transfers between devices with their start and end apart: 6, of which 5 were waited for; matrix products, arithmetic and copies ran while one was open for 13% of the time, Pallas kernels for 0%

commit v1 on v0

--- a/solution.py
+++ b/solution.py
@@ -1,8 +1,11 @@
+import functools
 import math
 
 import jax
 import jax.numpy as jnp
 from jax import lax
+from jax.experimental import pallas as pl
+from jax.experimental.pallas import tpu as pltpu
 from jax.sharding import PartitionSpec as P
 
 HEADS = 12
@@ -93,7 +96,7 @@
     return (attended, logsum)
 
 
-def per_device(queries, key_rows, value_rows, counts, head_of, out_weight):
+def per_device_exchange(queries, key_rows, value_rows, counts, head_of, out_weight):
     seq_count = lax.axis_size("seq")
     tok_dev = queries.shape[1]
     slot_count = head_of.shape[1]
@@ -159,9 +162,182 @@
     return (projected, saved_rows)
 
 
+CLIP_AXES = ("seq", "branch")
+KERNEL_PARAMS = pltpu.CompilerParams(vmem_limit_bytes=16 * 1024 * 1024)
+
+
+def clip_position():
+    return lax.axis_index("seq"), lax.axis_index("branch")
+
+
+def swap_with(array, offset, device_count):
+    return lax.ppermute(array, CLIP_AXES, [(i, i ^ offset) for i in range(device_count)])
+
+
+def pack_kernel(device_count, head_ref, query_ref, key_ref, value_ref, *message_refs):
+    shard, core = clip_position()
+    tok_dev = query_ref.shape[1]
+    for offset in range(device_count):
+        head = head_ref[core ^ (offset % 2), shard ^ (offset // 2)]
+        columns = pl.ds(pl.multiple_of(head * HDIM, HDIM), HDIM)
+        for part, source_ref in enumerate((query_ref, key_ref, value_ref)):
+            message_refs[offset][pl.ds(part * tok_dev, tok_dev), :] = source_ref[0, :, columns]
+
+
+def attend_kernel(device_count, head_ref, counts_ref, *refs):
+    message_refs = refs[:device_count]
+    guided_refs = refs[device_count : device_count + device_count // 2]
+    own_tile_ref, other_tile_ref = refs[device_count + device_count // 2 :]
+    shard_count = device_count // 2
+    shard, core = clip_position()
+    tok_dev = message_refs[0].shape[0] // 3
+    tokens = shard_count * tok_dev
+    row_cap = own_tile_ref.shape[1]
+    shard_tokens = [counts_ref[shard ^ block] for block in range(shard_count)]
+
+    lane = lax.broadcasted_iota(jnp.int32, (1, tokens), 1)
+    lane_block = lane // tok_dev
+    lane_limit = jnp.zeros((1, tokens), jnp.int32)
+    for block in range(shard_count):
+        lane_limit = jnp.where(lane_block == block, shard_tokens[block], lane_limit)
+    key_valid = lane - lane_block * tok_dev < lane_limit
+
+    scale_factor = 1.0 / math.sqrt(HDIM)
+    attended = []
+    logsums = []
+    for side in range(2):
+        sides = [message_refs[2 * block + side] for block in range(shard_count)]
+
+        def gathered(part):
+            return jnp.concatenate(
+                [ref[pl.ds(part * tok_dev, tok_dev), :] for ref in sides], axis=0
+            )
+
+        scores = (
+            lax.dot_general(
+                gathered(0),
+                gathered(1),
+                (((1,), (1,)), ((), ())),
+                preferred_element_type=jnp.float32,
+            )
+            * scale_factor
+        )
+        scores = jnp.where(key_valid, scores, -jnp.inf)
+        top_score = jnp.max(scores, axis=1, keepdims=True)
+        weights = jnp.exp(scores - top_score)
+        weight_sum = jnp.sum(weights, axis=1, keepdims=True)
+        mixed = jnp.dot(
+            weights.astype(jnp.bfloat16), gathered(2), preferred_element_type=jnp.float32
+        )
+        attended.append((mixed / weight_sum).astype(jnp.bfloat16).astype(jnp.float32))
+        logsums.append(top_score + jnp.log(weight_sum))
+
+    own_scale = jnp.where(core == 0, GUIDE_SCALE, 1.0 - GUIDE_SCALE)
+    other_scale = jnp.where(core == 0, 1.0 - GUIDE_SCALE, GUIDE_SCALE)
+    guided = own_scale * attended[0] + other_scale * attended[1]
+    row = lax.broadcasted_iota(jnp.int32, (tok_dev, HDIM), 0)
+    for block in range(shard_count):
+        rows = guided[block * tok_dev : (block + 1) * tok_dev]
+        rows = jnp.where(row < shard_tokens[block], rows, 0.0)
+        guided_refs[block][...] = rows.astype(jnp.bfloat16)
+
+    my_head = head_ref[core, shard]
+    group_size = jnp.int32(0)
+    group_rank = jnp.int32(0)
+    for other_shard in range(head_ref.shape[1]):
+        for other_core in range(head_ref.shape[0]):
+            same = (head_ref[other_core, other_shard] == my_head).astype(jnp.int32)
+            earlier = (other_shard * 2 + other_core < shard * 2 + core).astype(jnp.int32)
+            group_size = group_size + same
+            group_rank = group_rank + same * earlier
+    token = lax.broadcasted_iota(jnp.int32, (tok_dev, row_cap), 0)
+    step = lax.broadcasted_iota(jnp.int32, (tok_dev, row_cap), 1)
+    served = group_rank + group_size * step
+    for side, tile_ref in enumerate((own_tile_ref, other_tile_ref)):
+        for block in range(shard_count):
+            taken = (token == served) & (served < shard_tokens[block])
+            column = logsums[side][block * tok_dev : (block + 1) * tok_dev]
+            line = jnp.sum(jnp.where(taken, column, 0.0), axis=0, keepdims=True)
+            tile_ref[pl.ds(shard ^ block, 1), :] = line
+
+
+def project_kernel(device_count, head_ref, weight_ref, own_tile_ref, other_tile_ref, *refs):
+    message_refs = refs[:device_count]
+    projected_ref, saved_ref, guided_ref = refs[device_count:]
+    shard, core = clip_position()
+    saved_ref[core] = own_tile_ref[...]
+    saved_ref[1 - core] = other_tile_ref[...]
+    for offset in range(device_count):
+        head = head_ref[core ^ (offset % 2), shard ^ (offset // 2)]
+        columns = pl.ds(pl.multiple_of(head * HDIM, HDIM), HDIM)
+        guided_ref[:, columns] = message_refs[offset][...]
+    guided = guided_ref[...]
+    magnitude = jnp.mean(jnp.abs(guided.astype(jnp.float32)), axis=1, keepdims=True)
+    total = jnp.dot(guided, weight_ref[...], preferred_element_type=jnp.float32)
+    projected_ref[...] = (total / (magnitude + EPSILON)).astype(jnp.bfloat16)
+
+
+def per_device_direct(queries, key_rows, value_rows, counts, head_of, out_weight):
+    seq_count = lax.axis_size("seq")
+    device_count = seq_count * lax.axis_size("branch")
+    tok_dev = queries.shape[1]
+    slot_count = head_of.shape[1]
+    fewest = max(1, seq_count * slot_count // (2 * HEADS))
+    row_cap = (tok_dev + fewest - 1) // fewest
+    head_table = jnp.transpose(head_of)
+    smem = pl.BlockSpec(memory_space=pltpu.SMEM)
+    vmem = pl.BlockSpec(memory_space=pltpu.VMEM)
+
+    def held(array):
+        return pltpu.with_memory_space_constraint(array, pltpu.VMEM)
+
+    messages = pl.pallas_call(
+        functools.partial(pack_kernel, device_count),
+        out_shape=[pltpu.VMEM((3 * tok_dev, HDIM), jnp.bfloat16)] * device_count,
+        in_specs=[smem] + [vmem] * 3,
+        out_specs=[vmem] * device_count,
+        compiler_params=KERNEL_PARAMS,
+        name="pack",
+    )(head_table, queries, key_rows, value_rows)
+    arrived = [messages[0]] + [
+        swap_with(messages[offset], offset, device_count) for offset in range(1, device_count)
+    ]
+    results = pl.pallas_call(
+        functools.partial(attend_kernel, device_count),
+        out_shape=[pltpu.VMEM((tok_dev, HDIM), jnp.bfloat16)] * seq_count
+        + [pltpu.VMEM((seq_count, row_cap), jnp.float32)] * 2,
+        in_specs=[smem] * 2 + [vmem] * device_count,
+        out_specs=[vmem] * (seq_count + 2),
+        compiler_params=KERNEL_PARAMS,
+        name="attend",
+    )(head_table, counts, *[held(message) for message in arrived])
+    guided = results[:seq_count]
+    own_tile, lent_tile = results[seq_count:]
+    returned = [guided[0]] + [
+        swap_with(guided[offset // 2], offset, device_count) for offset in range(1, device_count)
+    ]
+    other_tile = swap_with(lent_tile, 1, device_count)
+    projected, saved = pl.pallas_call(
+        functools.partial(project_kernel, device_count),
+        out_shape=[
+            jax.ShapeDtypeStruct((tok_dev, out_weight.shape[1]), jnp.bfloat16),
+            jax.ShapeDtypeStruct((slot_count, seq_count, row_cap), jnp.float32),
+        ],
+        in_specs=[smem] + [vmem] * (3 + device_count),
+        out_specs=[vmem] * 2,
+        scratch_shapes=[pltpu.VMEM((tok_dev, HEADS * HDIM), jnp.bfloat16)],
+        compiler_params=KERNEL_PARAMS,
+        name="project",
+    )(head_table, held(out_weight), held(own_tile), held(other_tile), *[held(r) for r in returned])
+    saved = jnp.transpose(saved, (0, 2, 1))
+    return (projected, saved.reshape(1, 1, slot_count, row_cap, seq_count))
+
+
 def solution(mesh):
+    seq_count = mesh.shape["seq"]
+    few_devices = seq_count & (seq_count - 1) == 0 and seq_count <= HEADS
     return jax.shard_map(
-        per_device,
+        per_device_direct if few_devices else per_device_exchange,
         mesh=mesh,
         in_specs=(
             P("branch", ("groups", "seq"), None),

time: 71.1 us -> 60.7 us (0.85)
  starting transfers between devices: 23.3 us -> 43.1 us
  waiting for transfers between devices: 26.3 us -> 7.85 us
  local copies, waits for them, and re-layouts: 12.6 us -> 5.39 us
  other arithmetic: 5.54 us -> 0 us
  Pallas kernels: 0 us -> 3.39 us
  matrix products: 1.82 us -> 0 us
    ppermute x1 -> x31, starting transfers between devices: 0.07 us -> 43.1 us  [swap_with(): lax.ppermute(array, CLIP_AXES, [(i, i ^ offset) for i in range(device_cou...]
    all_to_all x5 -> x0, waiting for transfers between devices: 25.1 us -> none  [the longest x1 6.9 us: per_device(): lax.all_to_all(key_send, 'seq', split_axis=0, concat_axis=0, tiled=True)]
    all_to_all x5 -> x0, starting transfers between devices: 23.3 us -> none  [the longest x1 7.25 us: per_device(): lax.all_to_all(query_send, 'seq', split_axis=0, concat_axis=0, tiled=True)]
    gather x4 -> x0, local copies, waits for them, and re-layouts: 6.79 us -> none  [the longest x1 2.21 us: per_device(): value_grid[token_ids[None, :], flat_heads[:, None]]]
    ppermute x1 -> x31, waiting for transfers between devices: 1.21 us -> 7.85 us  [swap_with(): lax.ppermute(array, CLIP_AXES, [(i, i ^ offset) for i in range(device_cou...]
    unnamed x3 -> x12, local copies, waits for them, and re-layouts: 0.91 us -> 5.39 us
    pallas_call x0 -> x3, Pallas kernels: none -> 3.39 us  [the longest x1 1.61 us: per_device_direct(): pl.pallas_call(functools.partial(project_kernel, device_count), out_shape...]
    another operation x6 -> x0, local copies, waits for them, and re-layouts: 2.6 us -> none  [the longest x2 0.87 us: per_device(): query_grid = queries[0].reshape(tok_dev, HEADS, HDIM)]
  transfers between devices with their start and end apart: 6 -> 31, of which waited for: 5 -> 5; matrix products, arithmetic and copies ran while one was open for 13% -> 0% of each run, Pallas kernels for 0% -> 0%
where the time goes in v1:
time: 60.7 us; the launch traced here: 60.4 us
  starting transfers between devices  43.1 us (71%)
  waiting for transfers between devices  7.85 us (13%)
  local copies, waits for them, and re-layouts  5.39 us (9%)
  Pallas kernels  3.39 us (6%)
  between operations  0.7 us (1%)
    ppermute x31, starting transfers between devices, swap_with(): lax.ppermute(array, CLIP_AXES, [(i, i ^ offset) for i in range(device_cou...  43.1 us
    ppermute x31, waiting for transfers between devices, swap_with(): lax.ppermute(array, CLIP_AXES, [(i, i ^ offset) for i in range(device_cou...  7.85 us
    unnamed x12, local copies, waits for them, and re-layouts  5.39 us
    pallas_call x1, Pallas kernels, per_device_direct(): pl.pallas_call(functools.partial(project_kernel, device_count), out_shape...  1.61 us
  transfers between devices with their start and end apart: 31, of which 5 were waited for; matrix products, arithmetic and copies ran while one was open for 0% of the time, Pallas kernels for 0%

profile of v1, /device:TPU:0, one launch (start us, length us, event | category | flops | bytes accessed | tf_op | source)
XLA Modules:
  0.0 60.4 jit_solution(12018481841335933275)
XLA Ops:
  0.6 0.8 %copy-done.1 = bf16[1,16,1536]{2,1,0:T(8,128)(2,1)S(1)} copy-done((bf16[1,16,1536]{2,1,0:T(8,128)(2,1)S(1)}, bf16[1,16,1536]{2,1,0:T(8,128)(2,1)}, u32[]{:S(2)}) %copy-start.1) | copy-done | bytes 49176
  1.4 0.8 %copy-done.2 = bf16[1,16,1536]{2,1,0:T(8,128)(2,1)S(1)} copy-done((bf16[1,16,1536]{2,1,0:T(8,128)(2,1)S(1)}, bf16[1,16,1536]{2,1,0:T(8,128)(2,1)}, u32[]{:S(2)}) %copy-start.2) | copy-done | bytes 49176
  2.2 0.8 %copy-done.3 = bf16[1,16,1536]{2,1,0:T(8,128)(2,1)S(1)} copy-done((bf16[1,16,1536]{2,1,0:T(8,128)(2,1)S(1)}, bf16[1,16,1536]{2,1,0:T(8,128)(2,1)}, u32[]{:S(2)}) %copy-start.3) | copy-done | bytes 49176
  3.0 0.7 %copy-done.4 = s32[8,2]{0,1:T(2,128)S(1)} copy-done((s32[8,2]{0,1:T(2,128)S(1)}, s32[8,2]{0,1:T(2,128)}, u32[]{:S(2)}) %copy-start.4) | copy-done | bytes 88
  3.7 0.6 %pack.1 = (bf16[48,128]{1,0:T(8,128)(2,1)S(1)}, bf16[48,128]{1,0:T(8,128)(2,1)S(1)}, bf16[48,128]{1,0:T(8,128)(2,1)S(1)}, bf16[48,128]{1,0:T(8,128)(2,1)S(1)}, b...) custom-call(s32[2,8]{1,0:T(2,128)S(1)} %bitcast.4, ...), custom_call_target="tpu_custom_call" | custom-call | tf_op jit(solution)/shard_map/pack/pallas_call | solution.py:294
  4.3 0.5 collective-permute-start
  4.9 2.6 %collective-permute-start.1 = (bf16[48,128]{1,0:T(8,128)(2,1)S(1)}, bf16[48,128]{1,0:T(8,128)(2,1)S(1)}, u32[]{:S(2)}, u32[]{:S(2)}) collective-permute-start(bf16[48,128]{1,0:T(8,128)(2,1)S(1)} %get-tuple-element.32), channel_id=1, source_target_pairs={{0,2},{1,3},{2,0},{3,1},{4,6},{5,7},{6,4},{7,5},{8,10},{9,11},{10,... | collective-permute-start | bytes 36872 | tf_op jit(solution)/shard_map/ppermute | solution.py:174
  7.4 0.1 collective-permute-start.2
  7.5 1.8 %collective-permute-start.3 = (bf16[48,128]{1,0:T(8,128)(2,1)S(1)}, bf16[48,128]{1,0:T(8,128)(2,1)S(1)}, u32[]{:S(2)}, u32[]{:S(2)}) collective-permute-start(bf16[48,128]{1,0:T(8,128)(2,1)S(1)} %get-tuple-element.34), channel_id=1, source_target_pairs={{0,4},{1,5},{2,6},{3,7},{4,0},{5,1},{6,2},{7,3},{8,12},{9,13},{10,... | collective-permute-start | bytes 36872 | tf_op jit(solution)/shard_map/ppermute | solution.py:174
  9.3 0.0 collective-permute-start.4
  9.3 0.0 collective-permute-done.refs_1_
  9.3 2.6 %collective-permute-start.5 = (bf16[48,128]{1,0:T(8,128)(2,1)S(1)}, bf16[48,128]{1,0:T(8,128)(2,1)S(1)}, u32[]{:S(2)}, u32[]{:S(2)}) collective-permute-start(bf16[48,128]{1,0:T(8,128)(2,1)S(1)} %get-tuple-element.36), channel_id=1, source_target_pairs={{0,6},{1,7},{2,4},{3,5},{4,2},{5,3},{6,0},{7,1},{8,14},{9,15},{10,... | collective-permute-start | bytes 36872 | tf_op jit(solution)/shard_map/ppermute | solution.py:174
  11.9 0.0 collective-permute-done.1.refs_2_
  11.9 0.1 collective-permute-start.6
  12.1 0.0 collective-permute-done.2.refs_3_
  12.1 2.7 %collective-permute-start.7 = (bf16[48,128]{1,0:T(8,128)(2,1)S(1)}, bf16[48,128]{1,0:T(8,128)(2,1)S(1)}, u32[]{:S(2)}, u32[]{:S(2)}) collective-permute-start(bf16[48,128]{1,0:T(8,128)(2,1)S(1)} %get-tuple-element.38), channel_id=1, source_target_pairs={{0,8},{1,9},{2,10},{3,11},{4,12},{5,13},{6,14},{7,15},{8,0},{9,1},... | collective-permute-start | bytes 36872 | tf_op jit(solution)/shard_map/ppermute | solution.py:174
  14.7 0.0 collective-permute-done.3.refs_4_
  14.7 0.0 collective-permute-start.8
  14.8 0.0 collective-permute-done.4.refs_5_
  14.8 3.5 %collective-permute-start.9 = (bf16[48,128]{1,0:T(8,128)(2,1)S(1)}, bf16[48,128]{1,0:T(8,128)(2,1)S(1)}, u32[]{:S(2)}, u32[]{:S(2)}) collective-permute-start(bf16[48,128]{1,0:T(8,128)(2,1)S(1)} %get-tuple-element.40), channel_id=1, source_target_pairs={{0,10},{1,11},{2,8},{3,9},{4,14},{5,15},{6,12},{7,13},{8,2},{9,3},... | collective-permute-start | bytes 36872 | tf_op jit(solution)/shard_map/ppermute | solution.py:174
  18.3 0.0 collective-permute-done.5.refs_6_
  18.3 0.1 collective-permute-start.10
  18.4 0.0 collective-permute-done.6.refs_7_
  18.4 3.6 %collective-permute-start.11 = (bf16[48,128]{1,0:T(8,128)(2,1)S(1)}, bf16[48,128]{1,0:T(8,128)(2,1)S(1)}, u32[]{:S(2)}, u32[]{:S(2)}) collective-permute-start(bf16[48,128]{1,0:T(8,128)(2,1)S(1)} %get-tuple-element.42), channel_id=1, source_target_pairs={{0,12},{1,13},{2,14},{3,15},{4,8},{5,9},{6,10},{7,11},{8,4},{9,5},... | collective-permute-start | bytes 36872 | tf_op jit(solution)/shard_map/ppermute | solution.py:174
  21.9 0.0 collective-permute-done.7.refs_8_
  21.9 0.0 collective-permute-start.12
  22.0 0.0 collective-permute-done.8.refs_9_
  22.0 4.4 %collective-permute-start.13 = (bf16[48,128]{1,0:T(8,128)(2,1)S(1)}, bf16[48,128]{1,0:T(8,128)(2,1)S(1)}, u32[]{:S(2)}, u32[]{:S(2)}) collective-permute-start(bf16[48,128]{1,0:T(8,128)(2,1)S(1)} %get-tuple-element.44), channel_id=1, source_target_pairs={{0,14},{1,15},{2,12},{3,13},{4,10},{5,11},{6,8},{7,9},{8,6},{9,7},... | collective-permute-start | bytes 36872 | tf_op jit(solution)/shard_map/ppermute | solution.py:174
  26.4 0.0 collective-permute-done.9.refs_10_
  26.4 0.1 collective-permute-start.14
  26.5 0.0 collective-permute-done.10.refs_11_
  26.5 0.0 collective-permute-done.11.refs_12_
  26.5 0.4 collective-permute-done.12.refs_13_
  26.9 1.5 %collective-permute-done.13.refs_14_ = bf16[48,128]{1,0:T(8,128)(2,1)S(1)} collective-permute-done((bf16[48,128]{1,0:T(8,128)(2,1)S(1)}, bf16[48,128]{1,0:T(8,128)(2,1)S(1)}, u32[]{:S(2)}, u32[]{:S(2)}) %collective-permute-start.13) | collective-permute-done | bytes 12320 | tf_op jit(solution)/shard_map/ppermute | solution.py:174
  28.4 3.8 %collective-permute-done.14.refs_15_ = bf16[48,128]{1,0:T(8,128)(2,1)S(1)} collective-permute-done((bf16[48,128]{1,0:T(8,128)(2,1)S(1)}, bf16[48,128]{1,0:T(8,128)(2,1)S(1)}, u32[]{:S(2)}, u32[]{:S(2)}) %collective-permute-start.14) | collective-permute-done | bytes 12320 | tf_op jit(solution)/shard_map/ppermute | solution.py:174
  32.2 0.7 %copy-done.5 = s32[8]{0:T(128)S(1)} copy-done((s32[8]{0:T(128)S(1)}, s32[8]{0:T(128)}, u32[]{:S(2)}) %copy-start.5) | copy-done | bytes 56
  32.8 1.2 %attend.1 = (bf16[16,128]{1,0:T(8,128)(2,1)S(1)}, bf16[16,128]{1,0:T(8,128)(2,1)S(1)}, bf16[16,128]{1,0:T(8,128)(2,1)S(1)}, bf16[16,128]{1,0:T(8,128)(2,1)S(1)},...) custom-call(s32[2,8]{1,0:T(2,128)S(1)} %bitcast.5, ...), custom_call_target="tpu_custom_call" | custom-call | tf_op jit(solution)/shard_map/attend/pallas_call | solution.py:305
  34.0 0.2 collective-permute-start.15
  34.2 0.3 collective-permute-start.16
  34.6 0.3 collective-permute-start.18
  34.9 1.5 %collective-permute-start.17 = (bf16[16,128]{1,0:T(8,128)(2,1)S(1)}, bf16[16,128]{1,0:T(8,128)(2,1)S(1)}, u32[]{:S(2)}, u32[]{:S(2)}) collective-permute-start(bf16[16,128]{1,0:T(8,128)(2,1)S(1)} %get-tuple-element.49), channel_id=1, source_target_pairs={{0,2},{1,3},{2,0},{3,1},{4,6},{5,7},{6,4},{7,5},{8,10},{9,11},{10,... | collective-permute-start | bytes 12296 | tf_op jit(solution)/shard_map/ppermute | solution.py:174
  36.4 0.0 collective-permute-start.20
  36.4 0.0 collective-permute-done.15.other_tile_ref
  36.4 1.7 %collective-permute-start.19 = (bf16[16,128]{1,0:T(8,128)(2,1)S(1)}, bf16[16,128]{1,0:T(8,128)(2,1)S(1)}, u32[]{:S(2)}, u32[]{:S(2)}) collective-permute-start(bf16[16,128]{1,0:T(8,128)(2,1)S(1)} %get-tuple-element.50), channel_id=1, source_target_pairs={{0,4},{1,5},{2,6},{3,7},{4,0},{5,1},{6,2},{7,3},{8,12},{9,13},{10,... | collective-permute-start | bytes 12296 | tf_op jit(solution)/shard_map/ppermute | solution.py:174
  38.1 0.0 collective-permute-done.16.refs_1_
  38.1 0.1 collective-permute-start.22
  38.2 0.0 collective-permute-done.18.refs_3_
  38.2 2.6 %collective-permute-start.21 = (bf16[16,128]{1,0:T(8,128)(2,1)S(1)}, bf16[16,128]{1,0:T(8,128)(2,1)S(1)}, u32[]{:S(2)}, u32[]{:S(2)}) collective-permute-start(bf16[16,128]{1,0:T(8,128)(2,1)S(1)} %get-tuple-element.51), channel_id=1, source_target_pairs={{0,6},{1,7},{2,4},{3,5},{4,2},{5,3},{6,0},{7,1},{8,14},{9,15},{10,... | collective-permute-start | bytes 12296 | tf_op jit(solution)/shard_map/ppermute | solution.py:174
  40.8 0.0 collective-permute-done.17.refs_2_
  40.8 0.0 collective-permute-start.24
  40.8 0.0 collective-permute-done.20.refs_5_
  40.8 2.6 %collective-permute-start.23 = (bf16[16,128]{1,0:T(8,128)(2,1)S(1)}, bf16[16,128]{1,0:T(8,128)(2,1)S(1)}, u32[]{:S(2)}, u32[]{:S(2)}) collective-permute-start(bf16[16,128]{1,0:T(8,128)(2,1)S(1)} %get-tuple-element.52), channel_id=1, source_target_pairs={{0,8},{1,9},{2,10},{3,11},{4,12},{5,13},{6,14},{7,15},{8,0},{9,1},... | collective-permute-start | bytes 12296 | tf_op jit(solution)/shard_map/ppermute | solution.py:174
  43.4 0.0 collective-permute-done.19.refs_4_
  43.4 0.1 collective-permute-start.26
  43.5 0.0 collective-permute-done.22.refs_7_
  43.5 3.5 %collective-permute-start.25 = (bf16[16,128]{1,0:T(8,128)(2,1)S(1)}, bf16[16,128]{1,0:T(8,128)(2,1)S(1)}, u32[]{:S(2)}, u32[]{:S(2)}) collective-permute-start(bf16[16,128]{1,0:T(8,128)(2,1)S(1)} %get-tuple-element.53), channel_id=1, source_target_pairs={{0,10},{1,11},{2,8},{3,9},{4,14},{5,15},{6,12},{7,13},{8,2},{9,3},... | collective-permute-start | bytes 12296 | tf_op jit(solution)/shard_map/ppermute | solution.py:174
  47.0 0.1 collective-permute-start.28
  47.1 3.4 %collective-permute-start.27 = (bf16[16,128]{1,0:T(8,128)(2,1)S(1)}, bf16[16,128]{1,0:T(8,128)(2,1)S(1)}, u32[]{:S(2)}, u32[]{:S(2)}) collective-permute-start(bf16[16,128]{1,0:T(8,128)(2,1)S(1)} %get-tuple-element.54), channel_id=1, source_target_pairs={{0,12},{1,13},{2,14},{3,15},{4,8},{5,9},{6,10},{7,11},{8,4},{9,5},... | collective-permute-start | bytes 12296 | tf_op jit(solution)/shard_map/ppermute | solution.py:174
  50.5 0.3 collective-permute-start.30
  50.8 4.2 %collective-permute-start.29 = (bf16[16,128]{1,0:T(8,128)(2,1)S(1)}, bf16[16,128]{1,0:T(8,128)(2,1)S(1)}, u32[]{:S(2)}, u32[]{:S(2)}) collective-permute-start(bf16[16,128]{1,0:T(8,128)(2,1)S(1)} %get-tuple-element.55), channel_id=1, source_target_pairs={{0,14},{1,15},{2,12},{3,13},{4,10},{5,11},{6,8},{7,9},{8,6},{9,7},... | collective-permute-start | bytes 12296 | tf_op jit(solution)/shard_map/ppermute | solution.py:174
  55.0 1.2 %collective-permute-done.30.refs_15_ = bf16[16,128]{1,0:T(8,128)(2,1)S(1)} collective-permute-done((bf16[16,128]{1,0:T(8,128)(2,1)S(1)}, bf16[16,128]{1,0:T(8,128)(2,1)S(1)}, u32[]{:S(2)}, u32[]{:S(2)}) %collective-permute-start.30) | collective-permute-done | bytes 4128 | tf_op jit(solution)/shard_map/ppermute | solution.py:174
  56.2 0.9 %collective-permute-done.29.refs_14_ = bf16[16,128]{1,0:T(8,128)(2,1)S(1)} collective-permute-done((bf16[16,128]{1,0:T(8,128)(2,1)S(1)}, bf16[16,128]{1,0:T(8,128)(2,1)S(1)}, u32[]{:S(2)}, u32[]{:S(2)}) %collective-permute-start.29) | collective-permute-done | bytes 4128 | tf_op jit(solution)/shard_map/ppermute | solution.py:174
  57.1 1.7 %copy-done = bf16[1536,768]{1,0:T(8,128)(2,1)S(1)} copy-done((bf16[1536,768]{1,0:T(8,128)(2,1)S(1)}, bf16[1536,768]{1,0:T(8,128)(2,1)}, u32[]{:S(2)}) %copy-start) | copy-done | bytes 2359320
  58.8 1.6 %project.1 = (bf16[16,768]{1,0:T(8,128)(2,1)}, f32[2,8,16]{2,1,0:T(8,128)}) custom-call(s32[2,8]{1,0:T(2,128)S(1)} %bitcast.6, bf16[1536,768]{1,0:T(8,128)(2,1)S(1)} %copy-done, f32[8,16]{1,0:T(8,128)S(1)} %get-tuple-element.46.own_tile_ref, f32[8,16]{1,0:T(8,128)S(1)} %collective-permute-done.15.other_tile_ref, ...), custom_call_target="tpu_custom_call" | custom-call | tf_op jit(solution)/shard_map/project/pallas_call | solution.py:320
  (13 shorter events, 0.0 us)
Async XLA Ops:
  0.6 0.8 %copy-start.1 = (bf16[1,16,1536]{2,1,0:T(8,128)(2,1)S(1)}, bf16[1,16,1536]{2,1,0:T(8,128)(2,1)}, u32[]{:S(2)}) copy-start(bf16[1,16,1536]{2,1,0:T(8,128)(2,1)} %query_ref.1) | copy-start | bytes 147460
  1.4 0.8 %copy-start.2 = (bf16[1,16,1536]{2,1,0:T(8,128)(2,1)S(1)}, bf16[1,16,1536]{2,1,0:T(8,128)(2,1)}, u32[]{:S(2)}) copy-start(bf16[1,16,1536]{2,1,0:T(8,128)(2,1)} %key_ref.1) | copy-start | bytes 147460
  2.2 0.8 %copy-start.3 = (bf16[1,16,1536]{2,1,0:T(8,128)(2,1)S(1)}, bf16[1,16,1536]{2,1,0:T(8,128)(2,1)}, u32[]{:S(2)}) copy-start(bf16[1,16,1536]{2,1,0:T(8,128)(2,1)} %value_ref.1) | copy-start | bytes 147460
  3.0 0.7 %copy-start.4 = (s32[8,2]{0,1:T(2,128)S(1)}, s32[8,2]{0,1:T(2,128)}, u32[]{:S(2)}) copy-start(s32[8,2]{0,1:T(2,128)} %param.10) | copy-start | bytes 196
  4.3 5.0 %collective-permute-start = (bf16[48,128]{1,0:T(8,128)(2,1)S(1)}, bf16[48,128]{1,0:T(8,128)(2,1)S(1)}, u32[]{:S(2)}, u32[]{:S(2)}) collective-permute-start(bf16[48,128]{1,0:T(8,128)(2,1)S(1)} %get-tuple-element.31), channel_id=1, source_target_pairs={{0,1},{1,0},{2,3},{3,2},{4,5},{5,4},{6,7},{7,6},{8,9},{9,8},{10,11... | collective-permute-start | bytes 36872 | tf_op jit(solution)/shard_map/ppermute | solution.py:174
  4.9 7.1 %collective-permute-start.1 = (bf16[48,128]{1,0:T(8,128)(2,1)S(1)}, bf16[48,128]{1,0:T(8,128)(2,1)S(1)}, u32[]{:S(2)}, u32[]{:S(2)}) collective-permute-start(bf16[48,128]{1,0:T(8,128)(2,1)S(1)} %get-tuple-element.32), channel_id=1, source_target_pairs={{0,2},{1,3},{2,0},{3,1},{4,6},{5,7},{6,4},{7,5},{8,10},{9,11},{10,... | collective-permute-start | bytes 36872 | tf_op jit(solution)/shard_map/ppermute | solution.py:174
  7.4 4.6 %collective-permute-start.2 = (bf16[48,128]{1,0:T(8,128)(2,1)S(1)}, bf16[48,128]{1,0:T(8,128)(2,1)S(1)}, u32[]{:S(2)}, u32[]{:S(2)}) collective-permute-start(bf16[48,128]{1,0:T(8,128)(2,1)S(1)} %get-tuple-element.33), channel_id=1, source_target_pairs={{0,3},{1,2},{2,1},{3,0},{4,7},{5,6},{6,5},{7,4},{8,11},{9,10},{10,... | collective-permute-start | bytes 36872 | tf_op jit(solution)/shard_map/ppermute | solution.py:174
  7.5 7.2 %collective-permute-start.3 = (bf16[48,128]{1,0:T(8,128)(2,1)S(1)}, bf16[48,128]{1,0:T(8,128)(2,1)S(1)}, u32[]{:S(2)}, u32[]{:S(2)}) collective-permute-start(bf16[48,128]{1,0:T(8,128)(2,1)S(1)} %get-tuple-element.34), channel_id=1, source_target_pairs={{0,4},{1,5},{2,6},{3,7},{4,0},{5,1},{6,2},{7,3},{8,12},{9,13},{10,... | collective-permute-start | bytes 36872 | tf_op jit(solution)/shard_map/ppermute | solution.py:174
  9.3 5.4 %collective-permute-start.4 = (bf16[48,128]{1,0:T(8,128)(2,1)S(1)}, bf16[48,128]{1,0:T(8,128)(2,1)S(1)}, u32[]{:S(2)}, u32[]{:S(2)}) collective-permute-start(bf16[48,128]{1,0:T(8,128)(2,1)S(1)} %get-tuple-element.35), channel_id=1, source_target_pairs={{0,5},{1,4},{2,7},{3,6},{4,1},{5,0},{6,3},{7,2},{8,13},{9,12},{10,... | collective-permute-start | bytes 36872 | tf_op jit(solution)/shard_map/ppermute | solution.py:174
  9.3 8.9 %collective-permute-start.5 = (bf16[48,128]{1,0:T(8,128)(2,1)S(1)}, bf16[48,128]{1,0:T(8,128)(2,1)S(1)}, u32[]{:S(2)}, u32[]{:S(2)}) collective-permute-start(bf16[48,128]{1,0:T(8,128)(2,1)S(1)} %get-tuple-element.36), channel_id=1, source_target_pairs={{0,6},{1,7},{2,4},{3,5},{4,2},{5,3},{6,0},{7,1},{8,14},{9,15},{10,... | collective-permute-start | bytes 36872 | tf_op jit(solution)/shard_map/ppermute | solution.py:174
  11.9 6.4 %collective-permute-start.6 = (bf16[48,128]{1,0:T(8,128)(2,1)S(1)}, bf16[48,128]{1,0:T(8,128)(2,1)S(1)}, u32[]{:S(2)}, u32[]{:S(2)}) collective-permute-start(bf16[48,128]{1,0:T(8,128)(2,1)S(1)} %get-tuple-element.37), channel_id=1, source_target_pairs={{0,7},{1,6},{2,5},{3,4},{4,3},{5,2},{6,1},{7,0},{8,15},{9,14},{10,... | collective-permute-start | bytes 36872 | tf_op jit(solution)/shard_map/ppermute | solution.py:174
  12.1 9.9 %collective-permute-start.7 = (bf16[48,128]{1,0:T(8,128)(2,1)S(1)}, bf16[48,128]{1,0:T(8,128)(2,1)S(1)}, u32[]{:S(2)}, u32[]{:S(2)}) collective-permute-start(bf16[48,128]{1,0:T(8,128)(2,1)S(1)} %get-tuple-element.38), channel_id=1, source_target_pairs={{0,8},{1,9},{2,10},{3,11},{4,12},{5,13},{6,14},{7,15},{8,0},{9,1},... | collective-permute-start | bytes 36872 | tf_op jit(solution)/shard_map/ppermute | solution.py:174
  14.7 7.3 %collective-permute-start.8 = (bf16[48,128]{1,0:T(8,128)(2,1)S(1)}, bf16[48,128]{1,0:T(8,128)(2,1)S(1)}, u32[]{:S(2)}, u32[]{:S(2)}) collective-permute-start(bf16[48,128]{1,0:T(8,128)(2,1)S(1)} %get-tuple-element.39), channel_id=1, source_target_pairs={{0,9},{1,8},{2,11},{3,10},{4,13},{5,12},{6,15},{7,14},{8,1},{9,0},... | collective-permute-start | bytes 36872 | tf_op jit(solution)/shard_map/ppermute | solution.py:174
  14.8 11.6 %collective-permute-start.9 = (bf16[48,128]{1,0:T(8,128)(2,1)S(1)}, bf16[48,128]{1,0:T(8,128)(2,1)S(1)}, u32[]{:S(2)}, u32[]{:S(2)}) collective-permute-start(bf16[48,128]{1,0:T(8,128)(2,1)S(1)} %get-tuple-element.40), channel_id=1, source_target_pairs={{0,10},{1,11},{2,8},{3,9},{4,14},{5,15},{6,12},{7,13},{8,2},{9,3},... | collective-permute-start | bytes 36872 | tf_op jit(solution)/shard_map/ppermute | solution.py:174
  18.3 8.2 %collective-permute-start.10 = (bf16[48,128]{1,0:T(8,128)(2,1)S(1)}, bf16[48,128]{1,0:T(8,128)(2,1)S(1)}, u32[]{:S(2)}, u32[]{:S(2)}) collective-permute-start(bf16[48,128]{1,0:T(8,128)(2,1)S(1)} %get-tuple-element.41), channel_id=1, source_target_pairs={{0,11},{1,10},{2,9},{3,8},{4,15},{5,14},{6,13},{7,12},{8,3},{9,2},... | collective-permute-start | bytes 36872 | tf_op jit(solution)/shard_map/ppermute | solution.py:174
  18.4 8.1 %collective-permute-start.11 = (bf16[48,128]{1,0:T(8,128)(2,1)S(1)}, bf16[48,128]{1,0:T(8,128)(2,1)S(1)}, u32[]{:S(2)}, u32[]{:S(2)}) collective-permute-start(bf16[48,128]{1,0:T(8,128)(2,1)S(1)} %get-tuple-element.42), channel_id=1, source_target_pairs={{0,12},{1,13},{2,14},{3,15},{4,8},{5,9},{6,10},{7,11},{8,4},{9,5},... | collective-permute-start | bytes 36872 | tf_op jit(solution)/shard_map/ppermute | solution.py:174
  21.9 4.9 %collective-permute-start.12 = (bf16[48,128]{1,0:T(8,128)(2,1)S(1)}, bf16[48,128]{1,0:T(8,128)(2,1)S(1)}, u32[]{:S(2)}, u32[]{:S(2)}) collective-permute-start(bf16[48,128]{1,0:T(8,128)(2,1)S(1)} %get-tuple-element.43), channel_id=1, source_target_pairs={{0,13},{1,12},{2,15},{3,14},{4,9},{5,8},{6,11},{7,10},{8,5},{9,4},... | collective-permute-start | bytes 36872 | tf_op jit(solution)/shard_map/ppermute | solution.py:174
  22.0 6.4 %collective-permute-start.13 = (bf16[48,128]{1,0:T(8,128)(2,1)S(1)}, bf16[48,128]{1,0:T(8,128)(2,1)S(1)}, u32[]{:S(2)}, u32[]{:S(2)}) collective-permute-start(bf16[48,128]{1,0:T(8,128)(2,1)S(1)} %get-tuple-element.44), channel_id=1, source_target_pairs={{0,14},{1,15},{2,12},{3,13},{4,10},{5,11},{6,8},{7,9},{8,6},{9,7},... | collective-permute-start | bytes 36872 | tf_op jit(solution)/shard_map/ppermute | solution.py:174
  26.4 5.8 %collective-permute-start.14 = (bf16[48,128]{1,0:T(8,128)(2,1)S(1)}, bf16[48,128]{1,0:T(8,128)(2,1)S(1)}, u32[]{:S(2)}, u32[]{:S(2)}) collective-permute-start(bf16[48,128]{1,0:T(8,128)(2,1)S(1)} %get-tuple-element.45), channel_id=1, source_target_pairs={{0,15},{1,14},{2,13},{3,12},{4,11},{5,10},{6,9},{7,8},{8,7},{9,6},... | collective-permute-start | bytes 36872 | tf_op jit(solution)/shard_map/ppermute | solution.py:174
  32.2 0.7 %copy-start.5 = (s32[8]{0:T(128)S(1)}, s32[8]{0:T(128)}, u32[]{:S(2)}) copy-start(s32[8]{0:T(128)} %counts_ref.1) | copy-start | bytes 100
  34.0 2.4 %collective-permute-start.15 = (f32[8,16]{1,0:T(8,128)S(1)}, f32[8,16]{1,0:T(8,128)S(1)}, u32[]{:S(2)}, u32[]{:S(2)}) collective-permute-start(f32[8,16]{1,0:T(8,128)S(1)} %get-tuple-element.47), channel_id=1, source_target_pairs={{0,1},{1,0},{2,3},{3,2},{4,5},{5,4},{6,7},{7,6},{8,9},{9,8},{10,11... | collective-permute-start | bytes 1544 | tf_op jit(solution)/shard_map/ppermute | solution.py:174
  34.2 3.8 %collective-permute-start.16 = (bf16[16,128]{1,0:T(8,128)(2,1)S(1)}, bf16[16,128]{1,0:T(8,128)(2,1)S(1)}, u32[]{:S(2)}, u32[]{:S(2)}) collective-permute-start(bf16[16,128]{1,0:T(8,128)(2,1)S(1)} %get-tuple-element.48.refs_0_), channel_id=1, source_target_pairs={{0,1},{1,0},{2,3},{3,2},{4,5},{5,4},{6,7},{7,6},{8,9},{9,8},{10,11... | collective-permute-start | bytes 12296 | tf_op jit(solution)/shard_map/ppermute | solution.py:174
  34.6 3.6 %collective-permute-start.18 = (bf16[16,128]{1,0:T(8,128)(2,1)S(1)}, bf16[16,128]{1,0:T(8,128)(2,1)S(1)}, u32[]{:S(2)}, u32[]{:S(2)}) collective-permute-start(bf16[16,128]{1,0:T(8,128)(2,1)S(1)} %get-tuple-element.49), channel_id=1, source_target_pairs={{0,3},{1,2},{2,1},{3,0},{4,7},{5,6},{6,5},{7,4},{8,11},{9,10},{10,... | collective-permute-start | bytes 12296 | tf_op jit(solution)/shard_map/ppermute | solution.py:174
  34.9 5.9 %collective-permute-start.17 = (bf16[16,128]{1,0:T(8,128)(2,1)S(1)}, bf16[16,128]{1,0:T(8,128)(2,1)S(1)}, u32[]{:S(2)}, u32[]{:S(2)}) collective-permute-start(bf16[16,128]{1,0:T(8,128)(2,1)S(1)} %get-tuple-element.49), channel_id=1, source_target_pairs={{0,2},{1,3},{2,0},{3,1},{4,6},{5,7},{6,4},{7,5},{8,10},{9,11},{10,... | collective-permute-start | bytes 12296 | tf_op jit(solution)/shard_map/ppermute | solution.py:174
  36.4 4.4 %collective-permute-start.20 = (bf16[16,128]{1,0:T(8,128)(2,1)S(1)}, bf16[16,128]{1,0:T(8,128)(2,1)S(1)}, u32[]{:S(2)}, u32[]{:S(2)}) collective-permute-start(bf16[16,128]{1,0:T(8,128)(2,1)S(1)} %get-tuple-element.50), channel_id=1, source_target_pairs={{0,5},{1,4},{2,7},{3,6},{4,1},{5,0},{6,3},{7,2},{8,13},{9,12},{10,... | collective-permute-start | bytes 12296 | tf_op jit(solution)/shard_map/ppermute | solution.py:174
  36.4 7.0 %collective-permute-start.19 = (bf16[16,128]{1,0:T(8,128)(2,1)S(1)}, bf16[16,128]{1,0:T(8,128)(2,1)S(1)}, u32[]{:S(2)}, u32[]{:S(2)}) collective-permute-start(bf16[16,128]{1,0:T(8,128)(2,1)S(1)} %get-tuple-element.50), channel_id=1, source_target_pairs={{0,4},{1,5},{2,6},{3,7},{4,0},{5,1},{6,2},{7,3},{8,12},{9,13},{10,... | collective-permute-start | bytes 12296 | tf_op jit(solution)/shard_map/ppermute | solution.py:174
  38.1 5.4 %collective-permute-start.22 = (bf16[16,128]{1,0:T(8,128)(2,1)S(1)}, bf16[16,128]{1,0:T(8,128)(2,1)S(1)}, u32[]{:S(2)}, u32[]{:S(2)}) collective-permute-start(bf16[16,128]{1,0:T(8,128)(2,1)S(1)} %get-tuple-element.51), channel_id=1, source_target_pairs={{0,7},{1,6},{2,5},{3,4},{4,3},{5,2},{6,1},{7,0},{8,15},{9,14},{10,... | collective-permute-start | bytes 12296 | tf_op jit(solution)/shard_map/ppermute | solution.py:174
  38.2 8.8 %collective-permute-start.21 = (bf16[16,128]{1,0:T(8,128)(2,1)S(1)}, bf16[16,128]{1,0:T(8,128)(2,1)S(1)}, u32[]{:S(2)}, u32[]{:S(2)}) collective-permute-start(bf16[16,128]{1,0:T(8,128)(2,1)S(1)} %get-tuple-element.51), channel_id=1, source_target_pairs={{0,6},{1,7},{2,4},{3,5},{4,2},{5,3},{6,0},{7,1},{8,14},{9,15},{10,... | collective-permute-start | bytes 12296 | tf_op jit(solution)/shard_map/ppermute | solution.py:174
  40.8 6.3 %collective-permute-start.24 = (bf16[16,128]{1,0:T(8,128)(2,1)S(1)}, bf16[16,128]{1,0:T(8,128)(2,1)S(1)}, u32[]{:S(2)}, u32[]{:S(2)}) collective-permute-start(bf16[16,128]{1,0:T(8,128)(2,1)S(1)} %get-tuple-element.52), channel_id=1, source_target_pairs={{0,9},{1,8},{2,11},{3,10},{4,13},{5,12},{6,15},{7,14},{8,1},{9,0},... | collective-permute-start | bytes 12296 | tf_op jit(solution)/shard_map/ppermute | solution.py:174
  40.8 9.7 %collective-permute-start.23 = (bf16[16,128]{1,0:T(8,128)(2,1)S(1)}, bf16[16,128]{1,0:T(8,128)(2,1)S(1)}, u32[]{:S(2)}, u32[]{:S(2)}) collective-permute-start(bf16[16,128]{1,0:T(8,128)(2,1)S(1)} %get-tuple-element.52), channel_id=1, source_target_pairs={{0,8},{1,9},{2,10},{3,11},{4,12},{5,13},{6,14},{7,15},{8,0},{9,1},... | collective-permute-start | bytes 12296 | tf_op jit(solution)/shard_map/ppermute | solution.py:174
  43.4 7.4 %collective-permute-start.26 = (bf16[16,128]{1,0:T(8,128)(2,1)S(1)}, bf16[16,128]{1,0:T(8,128)(2,1)S(1)}, u32[]{:S(2)}, u32[]{:S(2)}) collective-permute-start(bf16[16,128]{1,0:T(8,128)(2,1)S(1)} %get-tuple-element.53), channel_id=1, source_target_pairs={{0,11},{1,10},{2,9},{3,8},{4,15},{5,14},{6,13},{7,12},{8,3},{9,2},... | collective-permute-start | bytes 12296 | tf_op jit(solution)/shard_map/ppermute | solution.py:174
  43.5 11.5 %collective-permute-start.25 = (bf16[16,128]{1,0:T(8,128)(2,1)S(1)}, bf16[16,128]{1,0:T(8,128)(2,1)S(1)}, u32[]{:S(2)}, u32[]{:S(2)}) collective-permute-start(bf16[16,128]{1,0:T(8,128)(2,1)S(1)} %get-tuple-element.53), channel_id=1, source_target_pairs={{0,10},{1,11},{2,8},{3,9},{4,14},{5,15},{6,12},{7,13},{8,2},{9,3},... | collective-permute-start | bytes 12296 | tf_op jit(solution)/shard_map/ppermute | solution.py:174
  47.0 8.0 %collective-permute-start.28 = (bf16[16,128]{1,0:T(8,128)(2,1)S(1)}, bf16[16,128]{1,0:T(8,128)(2,1)S(1)}, u32[]{:S(2)}, u32[]{:S(2)}) collective-permute-start(bf16[16,128]{1,0:T(8,128)(2,1)S(1)} %get-tuple-element.54), channel_id=1, source_target_pairs={{0,13},{1,12},{2,15},{3,14},{4,9},{5,8},{6,11},{7,10},{8,5},{9,4},... | collective-permute-start | bytes 12296 | tf_op jit(solution)/shard_map/ppermute | solution.py:174
  47.1 7.9 %collective-permute-start.27 = (bf16[16,128]{1,0:T(8,128)(2,1)S(1)}, bf16[16,128]{1,0:T(8,128)(2,1)S(1)}, u32[]{:S(2)}, u32[]{:S(2)}) collective-permute-start(bf16[16,128]{1,0:T(8,128)(2,1)S(1)} %get-tuple-element.54), channel_id=1, source_target_pairs={{0,12},{1,13},{2,14},{3,15},{4,8},{5,9},{6,10},{7,11},{8,4},{9,5},... | collective-permute-start | bytes 12296 | tf_op jit(solution)/shard_map/ppermute | solution.py:174
  50.5 5.7 %collective-permute-start.30 = (bf16[16,128]{1,0:T(8,128)(2,1)S(1)}, bf16[16,128]{1,0:T(8,128)(2,1)S(1)}, u32[]{:S(2)}, u32[]{:S(2)}) collective-permute-start(bf16[16,128]{1,0:T(8,128)(2,1)S(1)} %get-tuple-element.55), channel_id=1, source_target_pairs={{0,15},{1,14},{2,13},{3,12},{4,11},{5,10},{6,9},{7,8},{8,7},{9,6},... | collective-permute-start | bytes 12296 | tf_op jit(solution)/shard_map/ppermute | solution.py:174
  50.8 6.3 %collective-permute-start.29 = (bf16[16,128]{1,0:T(8,128)(2,1)S(1)}, bf16[16,128]{1,0:T(8,128)(2,1)S(1)}, u32[]{:S(2)}, u32[]{:S(2)}) collective-permute-start(bf16[16,128]{1,0:T(8,128)(2,1)S(1)} %get-tuple-element.55), channel_id=1, source_target_pairs={{0,14},{1,15},{2,12},{3,13},{4,10},{5,11},{6,8},{7,9},{8,6},{9,7},... | collective-permute-start | bytes 12296 | tf_op jit(solution)/shard_map/ppermute | solution.py:174
  57.1 1.7 %copy-start = (bf16[1536,768]{1,0:T(8,128)(2,1)S(1)}, bf16[1536,768]{1,0:T(8,128)(2,1)}, u32[]{:S(2)}) copy-start(bf16[1536,768]{1,0:T(8,128)(2,1)} %weight_ref.1) | copy-start | bytes 7077892

commit v2 on v0

--- a/solution.py
+++ b/solution.py
@@ -1,8 +1,11 @@
+import functools
 import math
 
 import jax
 import jax.numpy as jnp
 from jax import lax
+from jax.experimental import pallas as pl
+from jax.experimental.pallas import tpu as pltpu
 from jax.sharding import PartitionSpec as P
 
 HEADS = 12
@@ -93,7 +96,7 @@
     return (attended, logsum)
 
 
-def per_device(queries, key_rows, value_rows, counts, head_of, out_weight):
+def per_device_exchange(queries, key_rows, value_rows, counts, head_of, out_weight):
     seq_count = lax.axis_size("seq")
     tok_dev = queries.shape[1]
     slot_count = head_of.shape[1]
@@ -159,7 +162,191 @@
     return (projected, saved_rows)
 
 
+KERNEL_PARAMS = pltpu.CompilerParams(vmem_limit_bytes=16 * 1024 * 1024)
+
+
+def softmax_parts(query_rows, key_all, key_valid):
+    scores = (
+        lax.dot_general(
+            query_rows, key_all, (((1,), (1,)), ((), ())), preferred_element_type=jnp.float32
+        )
+        * (1.0 / math.sqrt(HDIM))
+    )
+    scores = jnp.where(key_valid, scores, -jnp.inf)
+    top_score = jnp.max(scores, axis=1, keepdims=True)
+    weights = jnp.exp(scores - top_score)
+    weight_sum = jnp.sum(weights, axis=1, keepdims=True)
+    return top_score, weights, weight_sum
+
+
+def attend_kernel(
+    head_hbm,
+    counts_hbm,
+    query_hbm,
+    key_all_hbm,
+    value_all_hbm,
+    query_all_hbm,
+    weight_hbm,
+    attended_ref,
+    weight_out_ref,
+    saved_ref,
+    head_ref,
+    counts_ref,
+    query_ref,
+    key_all_ref,
+    value_all_ref,
+    query_all_ref,
+    copy_sems,
+):
+    copies = [
+        pltpu.make_async_copy(source, target, copy_sems.at[number])
+        for number, (source, target) in enumerate(
+            (
+                (counts_hbm, counts_ref),
+                (head_hbm, head_ref),
+                (query_hbm, query_ref),
+                (key_all_hbm, key_all_ref),
+                (value_all_hbm, value_all_ref),
+                (query_all_hbm, query_all_ref),
+                (weight_hbm, weight_out_ref),
+            )
+        )
+    ]
+    for copy in copies:
+        copy.start()
+    for copy in copies[:5]:
+        copy.wait()
+    shard = lax.axis_index("seq")
+    tokens = key_all_ref.shape[0]
+    tok_dev = query_ref.shape[1]
+    shard_count = tokens // tok_dev
+    slot_count, _, row_cap = saved_ref.shape
+    shard_tokens = [counts_ref[block] for block in range(shard_count)]
+
+    lane = lax.broadcasted_iota(jnp.int32, (1, tokens), 1)
+    lane_block = lane // tok_dev
+    lane_limit = jnp.zeros((1, tokens), jnp.int32)
+    for block in range(shard_count):
+        lane_limit = jnp.where(lane_block == block, shard_tokens[block], lane_limit)
+    key_valid = lane - lane_block * tok_dev < lane_limit
+
+    row_valid = lax.broadcasted_iota(jnp.int32, (tok_dev, HDIM), 0) < counts_ref[shard]
+    for head in range(HEADS):
+        columns = pl.ds(head * HDIM, HDIM)
+        _, weights, weight_sum = softmax_parts(
+            query_ref[0, :, columns], key_all_ref[:, columns], key_valid
+        )
+        mixed = jnp.dot(
+            weights.astype(jnp.bfloat16),
+            value_all_ref[:, columns],
+            preferred_element_type=jnp.float32,
+        )
+        rows = jnp.where(row_valid, mixed / weight_sum, 0.0)
+        attended_ref[:, columns] = rows.astype(jnp.bfloat16)
+
+    copies[5].wait()
+    token = lax.broadcasted_iota(jnp.int32, (tok_dev, row_cap), 0)
+    step = lax.broadcasted_iota(jnp.int32, (tok_dev, row_cap), 1)
+    for slot in range(slot_count):
+        head = head_ref[slot, shard]
+        group_size = jnp.int32(0)
+        group_rank = jnp.int32(0)
+        for other_shard in range(shard_count):
+            for other_slot in range(slot_count):
+                same = (head_ref[other_slot, other_shard] == head).astype(jnp.int32)
+                before = other_shard * slot_count + other_slot < shard * slot_count + slot
+                group_size = group_size + same
+                group_rank = group_rank + same * before.astype(jnp.int32)
+        columns = pl.ds(pl.multiple_of(head * HDIM, HDIM), HDIM)
+        top_score, _, weight_sum = softmax_parts(
+            query_all_ref[:, columns], key_all_ref[:, columns], key_valid
+        )
+        logsum = top_score + jnp.log(weight_sum)
+        served = group_rank + group_size * step
+        for block in range(shard_count):
+            taken = (token == served) & (served < shard_tokens[block])
+            column = logsum[block * tok_dev : (block + 1) * tok_dev]
+            saved_ref[slot, pl.ds(block, 1), :] = jnp.sum(
+                jnp.where(taken, column, 0.0), axis=0, keepdims=True
+            )
+    copies[6].wait()
+
+
+def project_kernel(own_ref, partner_ref, weight_ref, projected_ref):
+    on_positive = lax.axis_index("branch") == 0
+    own_scale = jnp.where(on_positive, GUIDE_SCALE, 1.0 - GUIDE_SCALE)
+    partner_scale = jnp.where(on_positive, 1.0 - GUIDE_SCALE, GUIDE_SCALE)
+    guided = own_scale * own_ref[...].astype(jnp.float32) + partner_scale * partner_ref[
+        ...
+    ].astype(jnp.float32)
+    magnitude = jnp.mean(jnp.abs(guided), axis=1, keepdims=True)
+    normed = (guided / (magnitude + EPSILON)).astype(jnp.bfloat16)
+    projected_ref[...] = jnp.dot(
+        normed, weight_ref[...], preferred_element_type=jnp.float32
+    ).astype(jnp.bfloat16)
+
+
+def per_device_gathered(queries, key_rows, value_rows, counts, head_of, out_weight):
+    seq_count = lax.axis_size("seq")
+    tok_dev = queries.shape[1]
+    tokens = seq_count * tok_dev
+    width = HEADS * HDIM
+    slot_count = head_of.shape[1]
+    fewest = max(1, seq_count * slot_count // (2 * HEADS))
+    row_cap = (tok_dev + fewest - 1) // fewest
+    vmem = pl.BlockSpec(memory_space=pltpu.VMEM)
+
+    query_all, key_all, value_all = [
+        lax.all_gather(array[0], "seq", axis=0, tiled=True)
+        for array in (queries, key_rows, value_rows)
+    ]
+    attended, weight_held, saved = pl.pallas_call(
+        attend_kernel,
+        out_shape=[
+            pltpu.VMEM((tok_dev, width), jnp.bfloat16),
+            pltpu.VMEM(out_weight.shape, jnp.bfloat16),
+            jax.ShapeDtypeStruct((slot_count, seq_count, row_cap), jnp.float32),
+        ],
+        in_specs=[pl.BlockSpec(memory_space=pl.ANY)] * 7,
+        out_specs=[vmem] * 3,
+        scratch_shapes=[
+            pltpu.SMEM((slot_count, seq_count), jnp.int32),
+            pltpu.SMEM((seq_count,), jnp.int32),
+            pltpu.VMEM((1, tok_dev, width), jnp.bfloat16),
+        ]
+        + [pltpu.VMEM((tokens, width), jnp.bfloat16)] * 3
+        + [pltpu.SemaphoreType.DMA((7,))],
+        compiler_params=KERNEL_PARAMS,
+        name="attend",
+    )(
+        *[
+            pltpu.with_memory_space_constraint(array, pltpu.HBM)
+            for array in (
+                jnp.transpose(head_of),
+                counts,
+                queries,
+                key_all,
+                value_all,
+                query_all,
+                out_weight,
+            )
+        ]
+    )
+    partner = partner_2(attended, "branch", 0)
+    projected = pl.pallas_call(
+        project_kernel,
+        out_shape=jax.ShapeDtypeStruct((tok_dev, out_weight.shape[1]), jnp.bfloat16),
+        in_specs=[vmem] * 3,
+        out_specs=vmem,
+        compiler_params=KERNEL_PARAMS,
+        name="project",
+    )(*[pltpu.with_memory_space_constraint(x, pltpu.VMEM) for x in (attended, partner, weight_held)])
+    saved = jnp.transpose(saved, (0, 2, 1))
+    return (projected, saved.reshape(1, 1, slot_count, row_cap, seq_count))
+
+
 def solution(mesh):
+    per_device = per_device_gathered if mesh.shape["seq"] <= HEADS else per_device_exchange
     return jax.shard_map(
         per_device,
         mesh=mesh,

time: 71.1 us -> 110 us (1.55)
  blocking collectives: 0 us -> 102 us
  waiting for transfers between devices: 26.3 us -> 1.22 us
  starting transfers between devices: 23.3 us -> 0.07 us
  local copies, waits for them, and re-layouts: 12.6 us -> 0 us
  Pallas kernels: 0 us -> 6.21 us
  other arithmetic: 5.54 us -> 0 us
  matrix products: 1.82 us -> 0 us
    all_gather x0 -> x3, blocking collectives: none -> 102 us  [per_device_gathered(): lax.all_gather(array[0], 'seq', axis=0, tiled=True)]
    all_to_all x5 -> x0, waiting for transfers between devices: 25.1 us -> none  [the longest x1 6.9 us: per_device(): lax.all_to_all(key_send, 'seq', split_axis=0, concat_axis=0, tiled=True)]
    all_to_all x5 -> x0, starting transfers between devices: 23.3 us -> none  [the longest x1 7.25 us: per_device(): lax.all_to_all(query_send, 'seq', split_axis=0, concat_axis=0, tiled=True)]
    gather x4 -> x0, local copies, waits for them, and re-layouts: 6.79 us -> none  [the longest x1 2.21 us: per_device(): value_grid[token_ids[None, :], flat_heads[:, None]]]
    pallas_call x0 -> x2, Pallas kernels: none -> 6.21 us  [the longest x1 5.1 us: per_device_gathered(): pl.pallas_call(attend_kernel, out_shape=[pltpu.VMEM((tok_dev, width), jnp...]
    another operation x6 -> x0, local copies, waits for them, and re-layouts: 2.6 us -> none  [the longest x2 0.87 us: per_device(): query_grid = queries[0].reshape(tok_dev, HEADS, HDIM)]
    convert_element_type x2 -> x0, other arithmetic: 2.05 us -> none  [the longest x1 1.32 us: per_device(): row_live.astype(jnp.bfloat16).reshape(seq_count, slot_count, row_cap)]
    dot_general x5 -> x0, matrix products: 1.82 us -> none  [the longest x1 1.08 us: per_device(): jnp.dot(normed, out_weight, preferred_element_type=jnp.float32)]
  transfers between devices with their start and end apart: 6 -> 1, of which waited for: 5 -> 1; matrix products, arithmetic and copies ran while one was open for 13% -> 0% of each run, Pallas kernels for 0% -> 0%
where the time goes in v2:
time: 110 us
  blocking collectives  102 us (93%)
  Pallas kernels  6.21 us (6%)
  waiting for transfers between devices  1.22 us (1%)
    all_gather x3, blocking collectives, per_device_gathered(): lax.all_gather(array[0], 'seq', axis=0, tiled=True)  102 us
    pallas_call x1, Pallas kernels, per_device_gathered(): pl.pallas_call(attend_kernel, out_shape=[pltpu.VMEM((tok_dev, width), jnp...  5.1 us
  transfers between devices with their start and end apart: 1, of which 1 were waited for; matrix products, arithmetic and copies ran while one was open for 0% of the time, Pallas kernels for 0%

profile of v2, /device:TPU:0, one launch (start us, length us, event | category | flops | bytes accessed | tf_op | source)
XLA Modules:
  0.0 109.8 jit_solution(7383508642200516951)
XLA Ops:
  0.6 35.2 %all-gather = bf16[1,128,1536]{2,1,0:T(8,128)(2,1)} all-gather(bf16[1,16,1536]{2,1,0:T(8,128)(2,1)} %param.7), channel_id=2, replica_groups=mesh['groups'=2,'seq'=8,'branch'=2] {'seq'}, dimensions={1}, use_global_device_ids=true | all-gather | bytes 442368 | tf_op jit(solution)/shard_map/all_gather | solution.py:300
  35.9 33.3 %all-gather.1 = bf16[1,128,1536]{2,1,0:T(8,128)(2,1)} all-gather(bf16[1,16,1536]{2,1,0:T(8,128)(2,1)} %param.8), channel_id=3, replica_groups=mesh['groups'=2,'seq'=8,'branch'=2] {'seq'}, dimensions={1}, use_global_device_ids=true | all-gather | bytes 442368 | tf_op jit(solution)/shard_map/all_gather | solution.py:300
  69.2 33.2 %all-gather.2 = bf16[1,128,1536]{2,1,0:T(8,128)(2,1)} all-gather(bf16[1,16,1536]{2,1,0:T(8,128)(2,1)} %query_hbm.1), channel_id=4, replica_groups=mesh['groups'=2,'seq'=8,'branch'=2] {'seq'}, dimensions={1}, use_global_device_ids=true | all-gather | bytes 442368 | tf_op jit(solution)/shard_map/all_gather | solution.py:300
  102.3 5.1 %attend.1 = (bf16[16,1536]{1,0:T(8,128)(2,1)S(1)}, bf16[1536,768]{1,0:T(8,128)(2,1)S(1)}, f32[2,8,16]{2,1,0:T(8,128)}) custom-call(s32[2,8]{1,0:T(2,128)} %bitcast.10, s32[8]{0:T(128)} %counts_hbm.1, bf16[1,16,1536]{2,1,0:T(8,128)(2,1)} %query_hbm.1, bf16[128,1536]{1,0:T(8,128)(2,1)} %bitcast.7, bf16[128,1536]{1,0:T(8,128)(2,1)} %bitcast.8, ...), custom_call_target="tpu_custom_call" | custom-call | tf_op jit(solution)/shard_map/attend/pallas_call | solution.py:303
  107.4 0.1 collective-permute-start
  107.5 1.2 %collective-permute-done.partner_ref = bf16[16,1536]{1,0:T(8,128)(2,1)S(1)} collective-permute-done((bf16[16,1536]{1,0:T(8,128)(2,1)S(1)}, bf16[16,1536]{1,0:T(8,128)(2,1)S(1)}, u32[]{:S(2)}, u32[]{:S(2)}) %collective-permute-start) | collective-permute-done | bytes 49184 | tf_op jit(solution)/shard_map/ppermute | solution.py:20
  108.7 1.1 %project.1 = bf16[16,768]{1,0:T(8,128)(2,1)} custom-call(bf16[16,1536]{1,0:T(8,128)(2,1)S(1)} %get-tuple-element.5.own_ref, bf16[16,1536]{1,0:T(8,128)(2,1)S(1)} %collective-permute-done.partner_ref, bf16[1536,768]{1,0:T(8,128)(2,1)S(1)} %get-tuple-element.6.weight_ref), custom_call_target="tpu_custom_call" | custom-call | tf_op jit(solution)/shard_map/project/pallas_call | solution.py:336
Async XLA Ops:
  107.4 1.3 %collective-permute-start = (bf16[16,1536]{1,0:T(8,128)(2,1)S(1)}, bf16[16,1536]{1,0:T(8,128)(2,1)S(1)}, u32[]{:S(2)}, u32[]{:S(2)}) collective-permute-start(bf16[16,1536]{1,0:T(8,128)(2,1)S(1)} %get-tuple-element.5.own_ref), channel_id=1, source_target_pairs={{0,1},{1,0},{2,3},{3,2},{4,5},{5,4},{6,7},{7,6},{8,9},{9,8},{10,11... | collective-permute-start | bytes 147464 | tf_op jit(solution)/shard_map/ppermute | solution.py:20
